TPU v7x, 512 devices: a whole 4x4x16 slice. The times are simulated.
512 devices in a mesh: dp: 16 (over x, z_hi), seq: 32 (over z_lo, y, core).
Axes of the slice: x: 4, y: 4, z: 16 (z_hi: 4, z_lo: 4; z = z_hi * 4 + z_lo), core: 2. Of those that a mesh axis runs over, the one named last changes fastest.
Arguments:
- queries: bfloat16 [16, 4096, 4096], P('dp', 'seq'), may hold values from -6 to 6
- key_rows: bfloat16 [16, 4096, 512], P('dp', 'seq'), may hold values from -6 to 6
- value_rows: bfloat16 [16, 4096, 512], P('dp', 'seq'), may hold values from -6 to 6
- out_grad: bfloat16 [16, 4096, 4096], P('dp', 'seq'), may hold values from -0.59765625 to 0.59765625
- log_norm: float32 [16, 4096, 32], P('dp', 'seq'), may hold values from 2 to 7
- row_delta: float32 [16, 4096, 32], P('dp', 'seq'), may hold values from -5 to 5
- doc_ids: int32 [16, 4096], P('dp', 'seq'), may hold values from 0 to 15, as said below
Outputs:
- query_grad: bfloat16 [16, 4096, 4096], P('dp', 'seq')
- key_grad: bfloat16 [16, 4096, 512], P('dp', 'seq')
- value_grad: bfloat16 [16, 4096, 512], P('dp', 'seq')
Inputs may be any that keep to these rules, and one draw needn't show every extreme that they name: `doc_ids`: in each sequence document numbers never fall and all 16 numbers occur. The sequence that stands p-th in an order drawn from the seed (p from 0) has a bound b = 4096 / 2 ** (1 + p % 4) on its documents' lengths, and one of its documents has exactly b tokens; so some sequence always holds a document of 2048 tokens, and where b = 256 every document has b tokens.
All inputs are finite; a program needn't handle non-finite values.
Results may differ from a plain program's by a relative error of at most 0.0026.
The roundings to bfloat16 on the way count: a program that leaves them out, or rounds other values in their place, can miss the bound.
Values may be sent and summed in bfloat16 or wider, within the bound.
A program may use at most 64 MiB of HBM per device.

v0:
```python
import jax
import jax.numpy as jnp
from jax import lax
from jax.sharding import PartitionSpec as P

KVH = 4
HDIM = 128


def from_partner(value, axis, apart):
    mask = 2**apart
    pairs = [(source, source ^ mask) for source in range(lax.axis_size(axis))]
    return lax.ppermute(value, axis, pairs)


def tile_loads(doc_all, q_tile, k_tile):
    length = doc_all.shape[0]
    first_docs = doc_all.reshape(length // q_tile, q_tile)[:, 0]
    last_docs = doc_all.reshape(length // k_tile, k_tile)[:, k_tile - 1]
    q_ends = jnp.arange(length // q_tile, dtype=jnp.int32) * q_tile + q_tile - 1
    k_starts = jnp.arange(length // k_tile, dtype=jnp.int32) * k_tile
    active = (k_starts[None, :] <= q_ends[:, None]) & (last_docs[None, :] >= first_docs[:, None])
    return jnp.sum(active.astype(jnp.int32))


def attend(
    q_rows,
    grad_rows,
    lse_rows,
    delta_rows,
    kv_rows,
    doc_q,
    doc_k,
    q_base,
    k_base,
    tile_limit,
    q_tile,
    k_tile,
):
    q_count = q_rows.shape[0]
    k_count = kv_rows.shape[0]
    heads = lse_rows.shape[1]
    head_dim = kv_rows.shape[1] // 2
    softmax_scale = head_dim ** (-0.5)
    q_three = q_rows.reshape(q_count, heads, head_dim)
    grad_three = grad_rows.reshape(q_count, heads, head_dim)
    offsets_q = jnp.arange(q_tile, dtype=jnp.int32)
    offsets_k = jnp.arange(k_tile, dtype=jnp.int32)

    def q_step(q_index, state_now):
        dq_acc, dkv_acc = state_now
        q_start = q_index * q_tile
        q_block = lax.dynamic_slice_in_dim(q_three, q_start, q_tile, 0)
        grad_block = lax.dynamic_slice_in_dim(grad_three, q_start, q_tile, 0)
        lse_block = lax.dynamic_slice_in_dim(lse_rows, q_start, q_tile, 0).T
        delta_block = lax.dynamic_slice_in_dim(delta_rows, q_start, q_tile, 0).T
        docs_block = lax.dynamic_slice_in_dim(doc_q, q_start, q_tile, 0)
        q_pos = q_base + q_start + offsets_q

        def k_step(k_index, tile_state):
            k_start = k_index * k_tile
            live = (
                (q_index < tile_limit)
                & (k_base + k_start <= q_base + q_start + q_tile - 1)
                & (doc_k[k_start + k_tile - 1] >= docs_block[0])
            )

            def compute(inputs):
                dq_tile, dkv_part = inputs
                kv_block = lax.dynamic_slice_in_dim(kv_rows, k_start, k_tile, 0)
                key_block = kv_block[:, :head_dim]
                value_block = kv_block[:, head_dim:]
                docs_keys = lax.dynamic_slice_in_dim(doc_k, k_start, k_tile, 0)
                k_pos = k_base + k_start + offsets_k
                key_mask = (docs_block[:, None] == docs_keys[None, :]) & (
                    k_pos[None, :] <= q_pos[:, None]
                )
                scores = (
                    jnp.einsum(
                        "qhd,kd->hqk", q_block, key_block, preferred_element_type=jnp.float32
                    )
                    * softmax_scale
                )
                attn_prob = jnp.where(key_mask[None], jnp.exp(scores - lse_block[:, :, None]), 0.0)
                prob_grad = jnp.einsum(
                    "qhd,kd->hqk", grad_block, value_block, preferred_element_type=jnp.float32
                )
                score_grad = attn_prob * (prob_grad - delta_block[:, :, None])
                prob_half = attn_prob.astype(jnp.bfloat16)
                score_half = score_grad.astype(jnp.bfloat16)
                value_part = jnp.einsum(
                    "hqk,qhd->kd", prob_half, grad_block, preferred_element_type=jnp.float32
                )
                key_part = jnp.einsum(
                    "hqk,qhd->kd", score_half, q_block, preferred_element_type=jnp.float32
                )
                dq_tile = dq_tile + jnp.einsum(
                    "hqk,kd->qhd", score_half, key_block, preferred_element_type=jnp.float32
                )
                previous = lax.dynamic_slice_in_dim(dkv_part, k_start, k_tile, 0)
                updated = previous + jnp.concatenate([key_part, value_part], axis=1)
                return (dq_tile, lax.dynamic_update_slice_in_dim(dkv_part, updated, k_start, 0))

            return lax.cond(live, compute, lambda unchanged: unchanged, tile_state)

        start_tile = (jnp.zeros((q_tile, heads, head_dim), jnp.float32), dkv_acc)
        dq_tile, dkv_acc = lax.fori_loop(0, k_count // k_tile, k_step, start_tile)
        dq_acc = lax.dynamic_update_slice_in_dim(
            dq_acc, dq_tile.reshape(q_tile, heads * head_dim), q_start, 0
        )
        return (dq_acc, dkv_acc)

    start_all = (
        jnp.zeros((q_count, heads * head_dim), jnp.float32),
        jnp.zeros((k_count, 2 * head_dim), jnp.float32),
    )
    return lax.fori_loop(0, q_count // q_tile, q_step, start_all)


def on_device(queries, key_rows, value_rows, out_grad, log_norm, row_delta, doc_ids):
    seq_count = lax.axis_size("seq")
    tokens_here = queries.shape[1]
    length = tokens_here * seq_count
    head_dim = HDIM
    kv_heads = KVH
    copies = seq_count // kv_heads
    keys_local = key_rows[0].reshape(tokens_here, kv_heads, 1, head_dim)
    values_local = value_rows[0].reshape(tokens_here, kv_heads, 1, head_dim)
    paired = jnp.concatenate([keys_local, values_local], axis=3)
    repeated = jnp.broadcast_to(paired, (tokens_here, kv_heads, copies, 2 * head_dim)).reshape(
        tokens_here, seq_count * 2 * head_dim
    )
    q_all, grad_all, kv_all = (
        lax.all_to_all(queries[0], "seq", split_axis=1, concat_axis=0, tiled=True),
        lax.all_to_all(out_grad[0], "seq", split_axis=1, concat_axis=0, tiled=True),
        lax.all_to_all(repeated, "seq", split_axis=1, concat_axis=0, tiled=True),
    )
    doc_copies = jnp.broadcast_to(doc_ids[0].astype(jnp.float32)[:, None], (tokens_here, seq_count))
    lse_all, delta_all, doc_float = (
        lax.all_to_all(log_norm[0], "seq", split_axis=1, concat_axis=0, tiled=True),
        lax.all_to_all(row_delta[0], "seq", split_axis=1, concat_axis=0, tiled=True),
        lax.all_to_all(doc_copies, "seq", split_axis=1, concat_axis=0, tiled=True),
    )
    doc_all = doc_float[:, 0].astype(jnp.int32)
    q_tile = min(512, length // 8)
    k_tile = q_tile // 2
    q_tiles = length // q_tile
    partner_bit = lax.axis_size("dp").bit_length() - 2
    quarter = length // 4
    my_load = tile_loads(doc_all, q_tile, k_tile).astype(jnp.float32)
    part_q, part_grad, part_kv = from_partner(
        (q_all[3 * quarter :], grad_all[3 * quarter :], kv_all[quarter:]), "dp", partner_bit
    )
    part_lse, part_delta, part_doc, part_load = from_partner(
        (lse_all[3 * quarter :], delta_all[3 * quarter :], doc_float, my_load.reshape(1)),
        "dp",
        partner_bit,
    )
    shipping = my_load > part_load[0]
    helping = part_load[0] > my_load
    own_limit = jnp.where(shipping, q_tiles - quarter // q_tile, q_tiles)
    dq_sum, dkv_sum = attend(
        q_all,
        grad_all,
        lse_all,
        delta_all,
        kv_all,
        doc_all,
        doc_all,
        0,
        0,
        own_limit,
        q_tile,
        k_tile,
    )
    partner_docs = part_doc[:, 0].astype(jnp.int32)
    help_limit = jnp.where(helping, quarter // q_tile, 0)
    dq_help, dkv_help = attend(
        part_q,
        part_grad,
        part_lse,
        part_delta,
        part_kv,
        partner_docs[3 * quarter :],
        partner_docs[quarter:],
        3 * quarter,
        quarter,
        help_limit,
        q_tile,
        k_tile,
    )
    dq_return, dkv_return = from_partner((dq_help, dkv_help), "dp", partner_bit)
    dq_sum = dq_sum.at[3 * quarter :].add(dq_return)
    dkv_sum = dkv_sum.at[quarter:].add(dkv_return)
    softmax_scale = head_dim ** (-0.5)
    dq_final = (dq_sum * softmax_scale).astype(jnp.bfloat16)
    dkv_scaled = jnp.concatenate(
        [dkv_sum[:, :head_dim] * softmax_scale, dkv_sum[:, head_dim:]], axis=1
    )
    query_back = lax.all_to_all(dq_final, "seq", split_axis=0, concat_axis=1, tiled=True)
    kv_back = lax.all_to_all(dkv_scaled, "seq", split_axis=0, concat_axis=1, tiled=True)
    summed = jnp.sum(kv_back.reshape(tokens_here, kv_heads, copies, 2 * head_dim), axis=2)
    key_grad = (
        summed[:, :, :head_dim].reshape(tokens_here, kv_heads * head_dim).astype(jnp.bfloat16)
    )
    value_grad = (
        summed[:, :, head_dim:].reshape(tokens_here, kv_heads * head_dim).astype(jnp.bfloat16)
    )
    return (query_back[None], key_grad[None], value_grad[None])


def solution(mesh):
    return jax.shard_map(
        on_device,
        mesh=mesh,
        in_specs=(
            P("dp", "seq", None),
            P("dp", "seq", None),
            P("dp", "seq", None),
            P("dp", "seq", None),
            P("dp", "seq", None),
            P("dp", "seq", None),
            P("dp", "seq"),
        ),
        out_specs=(P("dp", "seq", None), P("dp", "seq", None), P("dp", "seq", None)),
        check_vma=False,
    )
```

profile of v0, /device:TPU:28, one launch (start us, length us, event | category | flops | bytes accessed | tf_op | source)
XLA Modules:
  0.0 885.2 jit_solution(8895695039379394016)
XLA Ops:
  1.4 14.6 %all_to_all.137 = f32[128,32,1]{0,2,1:T(1,128)S(1)} all-to-all(f32[128,32,1]{0,2,1:T(1,128)S(1)} %broadcast_in_dim.35), channel_id=1, replica_groups=mesh['dp'=16,'seq'=32] {'seq'}, dimensions={1} | all-to-all | bytes 32768 | tf_op jit(solution)/shard_map/all_to_all | solution.py:142
  16.0 5.6 all-to-all-start.2
  27.4 5.7 all-to-all-start.1
  33.4 25.8 %all-to-all-done.1 = bf16[128,32,128]{0,2,1:T(8,128)(2,1)S(1)} async-done(((bf16[128,32,128]{0,2,1:T(8,128)(2,1)}), bf16[128,32,128]{0,2,1:T(8,128)(2,1)S(1)}, u32[]{:S(2)}, u32[]{:S(2)}) %all-to-all-start.1) | async-done | bytes 1048608 | tf_op jit(solution)/shard_map/all_to_all | solution.py:134
  60.7 5.8 all-to-all-start.5
  68.8 46.2 %all-to-all-done.5 = bf16[128,32,256]{2,0,1:T(8,128)(2,1)S(1)} async-done(((bf16[128,32,256]{2,0,1:T(8,128)(2,1)}), bf16[128,32,256]{2,0,1:T(8,128)(2,1)S(1)}, u32[]{:S(2)}, u32[]{:S(2)}) %all-to-all-start.5) | async-done | bytes 2097184 | tf_op jit(solution)/shard_map/all_to_all | solution.py:136
  115.0 6.1 all-to-all-start.3
  126.5 32.5 %collective-permute-start = (f32[1]{0:T(128)}, f32[1]{0:T(128)}, u32[]{:S(2)}, u32[]{:S(2)}) collective-permute-start(f32[1]{0:T(128)} %bitcast.42), channel_id=1, source_target_pairs={{0,256},{32,288},{64,320},{96,352},{128,384},{160,416},{192,448},{... | collective-permute-start | bytes 20 | tf_op jit(solution)/shard_map/ppermute | solution.py:13
  159.1 4.9 collective-permute-start.1
  164.0 7.7 all-to-all-start.4
  178.5 4.9 collective-permute-start.4
  185.9 4.9 collective-permute-start.5
  198.7 63.7 %while.139 = (s32[]{:T(128)}, f32[1024,128]{1,0:T(8,128)}, f32[3072,256]{0,1:T(8,128)}, s32[1024]{0:T(1024)S(1)}, bf16[1024,1,128]{2,0,1:T(8,128)(2,1)S(1)}, /*i...) while((s32[]{:T(128)}, f32[1024,128]{1,0:T(8,128)}, ...), condition=%wide.region_12.13_spmd.clone, body=%wide.region_7.12_spmd.clone.sunk | while | flops 169280288 | bytes 6518782 | solution.py:117
  199.7 29.9 %while.141 = (s32[]{:T(128)}, f32[512,1,128]{0,2,1:T(8,128)S(1)}, f32[3072,256]{0,1:T(8,128)}, s32[]{:T(128)}, pred[]{:T(512)}, /*index=5*/s32[3072]{0:T(1024)S(...) while((s32[]{:T(128)}, f32[512,1,128]{0,2,1:T(8,128)S(1)}, ...), condition=%wide.region_11.11_spmd, body=%wide.region_8.10_spmd.sunk | while | flops 169279760 | bytes 4667922 | solution.py:107
  231.6 29.9 %while.141 = (s32[]{:T(128)}, f32[512,1,128]{0,2,1:T(8,128)S(1)}, f32[3072,256]{0,1:T(8,128)}, s32[]{:T(128)}, pred[]{:T(512)}, /*index=5*/s32[3072]{0:T(1024)S(...) while((s32[]{:T(128)}, f32[512,1,128]{0,2,1:T(8,128)S(1)}, ...), condition=%wide.region_11.11_spmd, body=%wide.region_8.10_spmd.sunk | while | flops 169279760 | bytes 4667922 | solution.py:107
  262.4 35.7 %collective-permute-start.7 = (f32[1024,128]{1,0:T(8,128)}, f32[1024,128]{1,0:T(8,128)}, u32[]{:S(2)}, u32[]{:S(2)}) collective-permute-start(f32[1024,128]{1,0:T(8,128)} %get-tuple-element.2012), channel_id=1, source_target_pairs={{0,256},{32,288},{64,320},{96,352},{128,384},{160,416},{192,448},{... | collective-permute-start | bytes 1572872 | tf_op jit(solution)/shard_map/ppermute | solution.py:13
  307.6 435.4 %while.137 = (s32[]{:T(128)}, f32[4096,128]{1,0:T(8,128)}, f32[4096,256]{0,1:T(8,128)}, s32[4096]{0:T(1024)S(1)}, bf16[4096,1,128]{2,0,1:T(8,128)(2,1)}, /*index...) while((s32[]{:T(128)}, f32[4096,128]{1,0:T(8,128)}, ...), condition=%wide.region_6.7_spmd.clone, body=%wide.region_1.6_spmd.clone.sunk | while | flops 169280272 | bytes 6518706 | solution.py:117
  308.7 45.9 %while.140 = (s32[]{:T(128)}, f32[512,1,128]{0,2,1:T(8,128)S(1)}, f32[4096,256]{0,1:T(8,128)}, s32[]{:T(128)}, pred[]{:T(512)}, /*index=5*/s32[4096]{0:T(1024)S(...) while((s32[]{:T(128)}, f32[512,1,128]{0,2,1:T(8,128)S(1)}, ...), condition=%wide.region_5.5_spmd, body=%wide.region_2.4_spmd.sunk | while | flops 169279760 | bytes 4667890 | solution.py:107
  356.6 52.1 %while.140 = (s32[]{:T(128)}, f32[512,1,128]{0,2,1:T(8,128)S(1)}, f32[4096,256]{0,1:T(8,128)}, s32[]{:T(128)}, pred[]{:T(512)}, /*index=5*/s32[4096]{0:T(1024)S(...) while((s32[]{:T(128)}, f32[512,1,128]{0,2,1:T(8,128)S(1)}, ...), condition=%wide.region_5.5_spmd, body=%wide.region_2.4_spmd.sunk | while | flops 169279760 | bytes 4667890 | solution.py:107
  410.7 58.2 %while.140 = (s32[]{:T(128)}, f32[512,1,128]{0,2,1:T(8,128)S(1)}, f32[4096,256]{0,1:T(8,128)}, s32[]{:T(128)}, pred[]{:T(512)}, /*index=5*/s32[4096]{0:T(1024)S(...) while((s32[]{:T(128)}, f32[512,1,128]{0,2,1:T(8,128)S(1)}, ...), condition=%wide.region_5.5_spmd, body=%wide.region_2.4_spmd.sunk | while | flops 169279760 | bytes 4667890 | solution.py:107
  470.9 64.3 %while.140 = (s32[]{:T(128)}, f32[512,1,128]{0,2,1:T(8,128)S(1)}, f32[4096,256]{0,1:T(8,128)}, s32[]{:T(128)}, pred[]{:T(512)}, /*index=5*/s32[4096]{0:T(1024)S(...) while((s32[]{:T(128)}, f32[512,1,128]{0,2,1:T(8,128)S(1)}, ...), condition=%wide.region_5.5_spmd, body=%wide.region_2.4_spmd.sunk | while | flops 169279760 | bytes 4667890 | solution.py:107
  537.1 70.3 %while.140 = (s32[]{:T(128)}, f32[512,1,128]{0,2,1:T(8,128)S(1)}, f32[4096,256]{0,1:T(8,128)}, s32[]{:T(128)}, pred[]{:T(512)}, /*index=5*/s32[4096]{0:T(1024)S(...) while((s32[]{:T(128)}, f32[512,1,128]{0,2,1:T(8,128)S(1)}, ...), condition=%wide.region_5.5_spmd, body=%wide.region_2.4_spmd.sunk | while | flops 169279760 | bytes 4667890 | solution.py:107
  609.4 48.9 %while.140 = (s32[]{:T(128)}, f32[512,1,128]{0,2,1:T(8,128)S(1)}, f32[4096,256]{0,1:T(8,128)}, s32[]{:T(128)}, pred[]{:T(512)}, /*index=5*/s32[4096]{0:T(1024)S(...) while((s32[]{:T(128)}, f32[512,1,128]{0,2,1:T(8,128)S(1)}, ...), condition=%wide.region_5.5_spmd, body=%wide.region_2.4_spmd.sunk | while | flops 169279760 | bytes 4667890 | solution.py:107
  660.3 39.9 %while.140 = (s32[]{:T(128)}, f32[512,1,128]{0,2,1:T(8,128)S(1)}, f32[4096,256]{0,1:T(8,128)}, s32[]{:T(128)}, pred[]{:T(512)}, /*index=5*/s32[4096]{0:T(1024)S(...) while((s32[]{:T(128)}, f32[512,1,128]{0,2,1:T(8,128)S(1)}, ...), condition=%wide.region_5.5_spmd, body=%wide.region_2.4_spmd.sunk | while | flops 169279760 | bytes 4667890 | solution.py:107
  702.2 39.9 %while.140 = (s32[]{:T(128)}, f32[512,1,128]{0,2,1:T(8,128)S(1)}, f32[4096,256]{0,1:T(8,128)}, s32[]{:T(128)}, pred[]{:T(512)}, /*index=5*/s32[4096]{0:T(1024)S(...) while((s32[]{:T(128)}, f32[512,1,128]{0,2,1:T(8,128)S(1)}, ...), condition=%wide.region_5.5_spmd, body=%wide.region_2.4_spmd.sunk | while | flops 169279760 | bytes 4667890 | solution.py:107
  747.7 7.7 all-to-all-start.6
  755.5 5.6 copy.76
  761.1 4.9 fusion.58
  770.7 5.6 copy.77
  776.3 5.1 all-to-all-done.6
  781.4 5.9 all-to-all-start.7
  789.3 91.5 %all-to-all-done.7 = f32[32,128,256]{1,2,0:T(8,128)} async-done(((f32[32,128,256]{1,2,0:T(8,128)}), f32[32,128,256]{1,2,0:T(8,128)}, u32[]{:S(2)}, u32[]{:S(2)}) %all-to-all-start.7) | async-done | bytes 4194336 | tf_op jit(solution)/shard_map/all_to_all | solution.py:201
  (868 shorter events, 457.6 us)
Async XLA Ops:
  0.6 32.5 %copy-start = (bf16[1,128,512]{2,1,0:T(8,128)(2,1)S(1)}, bf16[1,128,512]{2,1,0:T(8,128)(2,1)}, u32[]{:S(2)}) copy-start(bf16[1,128,512]{2,1,0:T(8,128)(2,1)} %param.25) | copy-start | bytes 393220
  0.6 32.5 %copy-start.1 = (bf16[1,128,512]{2,1,0:T(8,128)(2,1)S(1)}, bf16[1,128,512]{2,1,0:T(8,128)(2,1)}, u32[]{:S(2)}) copy-start(bf16[1,128,512]{2,1,0:T(8,128)(2,1)} %param.24) | copy-start | bytes 393220
  16.0 11.5 %all-to-all-start.2 = ((f32[128,32,1]{0,2,1:T(1,128)}), f32[128,32,1]{0,2,1:T(1,128)S(1)}, u32[]{:S(2)}, u32[]{:S(2)}) async-start(f32[128,32,1]{0,2,1:T(1,128)} %bitcast.215), calls=%async_computation.2 | async-start | bytes 32768 | tf_op jit(solution)/shard_map/all_to_all | solution.py:140
  27.4 31.7 %all-to-all-start.1 = ((bf16[128,32,128]{0,2,1:T(8,128)(2,1)}), bf16[128,32,128]{0,2,1:T(8,128)(2,1)S(1)}, u32[]{:S(2)}, u32[]{:S(2)}) async-start(bf16[128,32,128]{0,2,1:T(8,128)(2,1)} %bitcast.30), calls=%async_computation.1 | async-start | bytes 2097152 | tf_op jit(solution)/shard_map/all_to_all | solution.py:134
  60.7 54.2 %all-to-all-start.5 = ((bf16[128,32,256]{2,0,1:T(8,128)(2,1)}), bf16[128,32,256]{2,0,1:T(8,128)(2,1)S(1)}, u32[]{:S(2)}, u32[]{:S(2)}) async-start(bf16[128,32,256]{2,0,1:T(8,128)(2,1)} %bitcast.192), calls=%async_computation.5 | async-start | bytes 4194304 | tf_op jit(solution)/shard_map/all_to_all | solution.py:136
  115.0 49.0 %all-to-all-start.3 = ((bf16[128,32,128]{0,2,1:T(8,128)(2,1)}), bf16[128,32,128]{0,2,1:T(8,128)(2,1)}, u32[]{:S(2)}, u32[]{:S(2)}) async-start(bf16[128,32,128]{0,2,1:T(8,128)(2,1)} %bitcast.195), calls=%async_computation.3 | async-start | bytes 2097152 | tf_op jit(solution)/shard_map/all_to_all | solution.py:135
  122.4 73.4 %collective-permute-start.6 = (bf16[3072,256]{1,0:T(8,128)(2,1)}, bf16[3072,256]{1,0:T(8,128)(2,1)}, u32[]{:S(2)}, u32[]{:S(2)}) collective-permute-start(bf16[3072,256]{1,0:T(8,128)(2,1)} %bitcast.58), channel_id=1, source_target_pairs={{0,256},{32,288},{64,320},{96,352},{128,384},{160,416},{192,448},{... | collective-permute-start | bytes 4718600 | tf_op jit(solution)/shard_map/ppermute | solution.py:13
  126.5 57.0 %collective-permute-start = (f32[1]{0:T(128)}, f32[1]{0:T(128)}, u32[]{:S(2)}, u32[]{:S(2)}) collective-permute-start(f32[1]{0:T(128)} %bitcast.42), channel_id=1, source_target_pairs={{0,256},{32,288},{64,320},{96,352},{128,384},{160,416},{192,448},{... | collective-permute-start | bytes 20 | tf_op jit(solution)/shard_map/ppermute | solution.py:13
  159.1 26.9 %collective-permute-start.1 = (f32[4096,1]{0,1:T(1,128)S(1)}, f32[4096,1]{0,1:T(1,128)S(1)}, u32[]{:S(2)}, u32[]{:S(2)}) collective-permute-start(f32[4096,1]{0,1:T(1,128)S(1)} %bitcast.205), channel_id=1, source_target_pairs={{0,256},{32,288},{64,320},{96,352},{128,384},{160,416},{192,448},{... | collective-permute-start | bytes 49160 | tf_op jit(solution)/shard_map/ppermute | solution.py:13
  164.0 19.5 %all-to-all-start.4 = ((f32[128,32,1]{0,2,1:T(1,128)}), f32[128,32,1]{0,2,1:T(1,128)S(1)}, u32[]{:S(2)}, u32[]{:S(2)}) async-start(f32[128,32,1]{0,2,1:T(1,128)} %bitcast.39), calls=%async_computation.4 | async-start | bytes 32768 | tf_op jit(solution)/shard_map/all_to_all | solution.py:141
  172.7 23.1 %collective-permute-start.2 = (bf16[1024,128]{1,0:T(8,128)(2,1)}, bf16[1024,128]{1,0:T(8,128)(2,1)S(1)}, u32[]{:S(2)}, u32[]{:S(2)}) collective-permute-start(bf16[1024,128]{1,0:T(8,128)(2,1)} %bitcast.202), channel_id=1, source_target_pairs={{0,256},{32,288},{64,320},{96,352},{128,384},{160,416},{192,448},{... | collective-permute-start | bytes 786440 | tf_op jit(solution)/shard_map/ppermute | solution.py:13
  178.5 17.3 %collective-permute-start.4 = (bf16[1024,128]{1,0:T(8,128)(2,1)}, bf16[1024,128]{1,0:T(8,128)(2,1)}, u32[]{:S(2)}, u32[]{:S(2)}) collective-permute-start(bf16[1024,128]{1,0:T(8,128)(2,1)} %bitcast.203), channel_id=1, source_target_pairs={{0,256},{32,288},{64,320},{96,352},{128,384},{160,416},{192,448},{... | collective-permute-start | bytes 786440 | tf_op jit(solution)/shard_map/ppermute | solution.py:13
  183.5 12.3 %collective-permute-start.3 = (f32[1024,1]{0,1:T(1,128)S(1)}, f32[1024,1]{0,1:T(1,128)S(1)}, u32[]{:S(2)}, u32[]{:S(2)}) collective-permute-start(f32[1024,1]{0,1:T(1,128)S(1)} %slice_bitcast_fusion.1), channel_id=1, source_target_pairs={{0,256},{32,288},{64,320},{96,352},{128,384},{160,416},{192,448},{... | collective-permute-start | bytes 12296 | tf_op jit(solution)/shard_map/ppermute | solution.py:13
  185.9 9.8 %collective-permute-start.5 = (f32[1024,1]{0,1:T(1,128)S(1)}, f32[1024,1]{0,1:T(1,128)S(1)}, u32[]{:S(2)}, u32[]{:S(2)}) collective-permute-start(f32[1024,1]{0,1:T(1,128)S(1)} %slice_bitcast_fusion), channel_id=1, source_target_pairs={{0,256},{32,288},{64,320},{96,352},{128,384},{160,416},{192,448},{... | collective-permute-start | bytes 12296 | tf_op jit(solution)/shard_map/ppermute | solution.py:13
  262.4 480.6 %collective-permute-start.7 = (f32[1024,128]{1,0:T(8,128)}, f32[1024,128]{1,0:T(8,128)}, u32[]{:S(2)}, u32[]{:S(2)}) collective-permute-start(f32[1024,128]{1,0:T(8,128)} %get-tuple-element.2012), channel_id=1, source_target_pairs={{0,256},{32,288},{64,320},{96,352},{128,384},{160,416},{192,448},{... | collective-permute-start | bytes 1572872 | tf_op jit(solution)/shard_map/ppermute | solution.py:13
  301.6 459.4 %collective-permute-start.8 = (f32[3072,256]{1,0:T(8,128)}, f32[3072,256]{1,0:T(8,128)}, u32[]{:S(2)}, u32[]{:S(2)}) collective-permute-start(f32[3072,256]{1,0:T(8,128)} %copy.75), channel_id=1, source_target_pairs={{0,256},{32,288},{64,320},{96,352},{128,384},{160,416},{192,448},{... | collective-permute-start | bytes 9437192 | tf_op jit(solution)/shard_map/ppermute | solution.py:13
  747.7 33.7 %all-to-all-start.6 = ((bf16[32,128,128]{2,1,0:T(8,128)(2,1)}), bf16[32,128,128]{2,1,0:T(8,128)(2,1)S(1)}, u32[]{:S(2)}, u32[]{:S(2)}) async-start(bf16[32,128,128]{2,1,0:T(8,128)(2,1)} %bitcast.59), calls=%async_computation.6 | async-start | bytes 2097152 | tf_op jit(solution)/shard_map/all_to_all | solution.py:200
  781.4 99.4 %all-to-all-start.7 = ((f32[32,128,256]{1,2,0:T(8,128)}), f32[32,128,256]{1,2,0:T(8,128)}, u32[]{:S(2)}, u32[]{:S(2)}) async-start(f32[32,128,256]{1,2,0:T(8,128)} %copy.77), calls=%async_computation.7 | async-start | bytes 8388608 | tf_op jit(solution)/shard_map/all_to_all | solution.py:201
where the time goes:
time: 892 us; the launch traced here: 885 us
  local copies, waits for them, and re-layouts  241 us (27%)
  loops' own time  202 us (23%)
  waiting for transfers between devices  172 us (19%)
  starting transfers between devices  137 us (15%)
  other arithmetic  76 us (9%)
  matrix products  40.1 us (4%)
  blocking collectives  14.6 us (2%)
    another operation x10, loops' own time, q_step(): dq_tile, dkv_acc = lax.fori_loop(0, k_count // k_tile, k_step, start_tile)  198 us
    dynamic_slice x152, local copies, waits for them, and re-layouts, k_step(): doc_k[k_start + k_tile - 1] >= docs_block[0]  101 us
    ppermute x9, starting transfers between devices, from_partner(): return lax.ppermute(value, axis, pairs)  92.2 us
    all_to_all x1, waiting for transfers between devices, on_device(): lax.all_to_all(dkv_scaled, 'seq', split_axis=0, concat_axis=1, tiled=True)  91.5 us
    slice x152, local copies, waits for them, and re-layouts, k_step(): docs_block[0]  76.6 us
    dynamic_update_slice x33, other arithmetic, compute(): lax.dynamic_update_slice_in_dim(dkv_part, updated, k_start, 0)  57.3 us
    all_to_all x1, waiting for transfers between devices, on_device(): lax.all_to_all(repeated, 'seq', split_axis=1, concat_axis=0, tiled=True)  46.2 us
    all_to_all x1, waiting for transfers between devices, on_device(): lax.all_to_all(queries[0], 'seq', split_axis=1, concat_axis=0, tiled=True)  25.8 us
  transfers between devices with their start and end apart: 16, of which 5 were waited for; matrix products, arithmetic and copies ran while one was open for 36% of the time, Pallas kernels for 0%

commit v1 on v0

v1 whole, which is shorter than its diff:
```python
import jax
import jax.numpy as jnp
from jax import lax
from jax.experimental import pallas as pl
from jax.experimental.pallas import tpu as pltpu
from jax.sharding import PartitionSpec as P

F32, BF16 = jnp.float32, jnp.bfloat16
HDIM = 128
TOK = 128
BLK = 2 * TOK
HEADS = 16
GROUP = 8
ROWS = GROUP * BLK
QC = 512
EXTRA = 16
NCH = 4
CH = BLK // NCH
SCALE = HDIM**-0.5
EXP_SCALE = SCALE * 1.4426950408889634
FAR = -1e30
ITEMS = ("k", "v", "doc", "lse", "delta", "q", "g")


def dot(a, b):
    return jnp.dot(a, b, preferred_element_type=F32)


def split3(x):
    hi = x.astype(BF16).astype(F32)
    mid = (x - hi).astype(BF16).astype(F32)
    return hi, mid, x - hi - mid


def kernel(
    q_in, k_in, v_in, g_in, lse_in, delta_in, doc_in,
    dq_out, dk_out, dv_out,
    kv, part_out, part_in, acc, zin, q_buf, g_buf, qt, gt, dqt, dq_half, fin, lse_buf, delta_buf, doc_buf,
    local_sem, x_send, x_recv, kv_send, kv_recv, kvz_send, p_send, p_recv, z_send, z_recv, f_send, f_recv, f_local,
):
    me = lax.axis_index("seq")
    core = me % 2
    y = (me // 2) % 4
    z = me // 8
    other = 1 - core

    def device(zz, yy, cc):
        return {"seq": (zz * 4 + yy) * 2 + cc}

    def remote(src, dst, send, recv, to):
        return pltpu.make_async_remote_copy(
            src_ref=src, dst_ref=dst, send_sem=send, recv_sem=recv, device_id=to, device_id_type=pl.DeviceIdType.MESH
        )

    sibling = device(z, y, other)
    down, up = device(z - 1, y, core), device(z + 1, y, core)

    def part_of(name, half):
        wide = pl.ds(pl.multiple_of(half * HEADS * HDIM, HEADS * HDIM), HEADS * HDIM)
        narrow = pl.ds(pl.multiple_of(half * 2 * HDIM, 2 * HDIM), 2 * HDIM)
        return {
            "q": lambda: q_in.at[:, wide],
            "g": lambda: g_in.at[:, wide],
            "k": lambda: k_in.at[:, narrow],
            "v": lambda: v_in.at[:, narrow],
            "lse": lambda: lse_in,
            "delta": lambda: delta_in,
            "doc": lambda: doc_in,
        }[name]()

    def place_of(name):
        rows = pl.ds(pl.multiple_of(core * TOK, TOK), TOK)
        return {
            "q": lambda: q_buf.at[rows],
            "g": lambda: g_buf.at[rows],
            "k": lambda: kv.at[0, y, rows, pl.ds(0, 2 * HDIM)],
            "v": lambda: kv.at[0, y, rows, pl.ds(2 * HDIM, 2 * HDIM)],
            "lse": lambda: lse_buf.at[rows],
            "delta": lambda: delta_buf.at[rows],
            "doc": lambda: doc_buf.at[core],
        }[name]()

    def local(name):
        return pltpu.make_async_copy(part_of(name, core), place_of(name), local_sem.at[ITEMS.index(name)])

    def swap(name):
        i = ITEMS.index(name)
        return remote(part_of(name, other), place_of(name), x_send.at[i], x_recv.at[i], sibling)

    for name in ITEMS:
        local(name).start()

    barrier = pltpu.get_barrier_semaphore()

    def greet(to):
        pl.semaphore_signal(barrier, inc=1, device_id=to, device_id_type=pl.DeviceIdType.MESH)

    greet(sibling)
    for apart in range(1, 4):
        greet(device(z, (y + apart) % 4, core))
    pl.when(z > 0)(lambda: greet(down))
    pl.when(z < 3)(lambda: greet(up))
    pl.semaphore_wait(barrier, 4 + (z + 3) // 4 + (6 - z) // 4)

    for name in ITEMS:
        swap(name).start()

    def arrive(name):
        local(name).wait()
        swap(name).wait_recv()

    def along_z(dz):
        return remote(kv.at[dz, y], kv.at[dz + 1, y], kvz_send.at[dz], kv_recv.at[dz + 1, y], up)

    def along_y(dz, to):
        return remote(kv.at[dz, y], kv.at[dz, y], kv_send.at[dz, to], kv_recv.at[dz, y], device(z, to, core))

    def arrived(dz, yk):
        remote(kv.at[dz, yk], kv.at[dz, yk], kv_send.at[dz, yk], kv_recv.at[dz, yk], sibling).wait_recv()

    def each_target(dz, act):
        for apart in range(1, 4):
            to = (y + apart) % 4
            if dz == 0:
                pl.when(to > y)(lambda to=to: act(to))
            elif dz == 1:
                act(to)
            else:
                pl.when(to < y)(lambda to=to: act(to))

    for name in ("k", "v", "doc"):
        arrive(name)
    docs = jnp.concatenate([doc_buf[0], doc_buf[1]], axis=1).astype(F32)
    docs16 = jnp.broadcast_to(docs, (EXTRA, BLK))
    kv[0, y, pl.ds(BLK, EXTRA), pl.ds(0, BLK)] = docs16.astype(BF16)
    kv[0, y, pl.ds(BLK, EXTRA), pl.ds(BLK, BLK)] = jnp.zeros((EXTRA, BLK), BF16)
    pl.when(z < 3)(lambda: along_z(0).start())
    each_target(0, lambda to: along_y(0, to).start())

    for name in ("lse", "delta", "q", "g"):
        arrive(name)
    sixteen = lax.broadcasted_iota(jnp.int32, (EXTRA, BLK), 0)
    bias = jnp.where(docs16 == sixteen.astype(F32), 0.0, FAR).astype(BF16)
    blank = jnp.zeros((EXTRA, BLK), BF16)
    zeros = jnp.zeros((HDIM - 2 * EXTRA, BLK), BF16)
    lse_t = jnp.where(core == 0, lse_buf[:, pl.ds(0, HEADS)], lse_buf[:, pl.ds(HEADS, HEADS)]).T
    delta_t = jnp.where(core == 0, delta_buf[:, pl.ds(0, HEADS)], delta_buf[:, pl.ds(HEADS, HEADS)]).T
    lse_parts = split3(lse_t * (-1.0 / SCALE))
    delta_parts = split3(-delta_t)
    for head in range(HEADS):
        h, cols = head // GROUP, pl.ds(head % GROUP * BLK, BLK)
        lanes = pl.ds(head * HDIM, HDIM)
        for source, out, first, top, parts in (
            (q_buf, qt, 0, bias, lse_parts), (g_buf, gt, 3, blank, delta_parts)
        ):
            rows = jnp.zeros((EXTRA, BLK), F32)
            for i, part in enumerate(parts):
                rows = jnp.where(sixteen == first + i, jnp.broadcast_to(part[head : head + 1], (EXTRA, BLK)), rows)
            out[h, pl.ds(0, HDIM), cols] = source[:, lanes].T
            out[h, pl.ds(HDIM, EXTRA), cols] = top
            out[h, pl.ds(HDIM + EXTRA, EXTRA), cols] = rows.astype(BF16)
            out[h, pl.ds(HDIM + 2 * EXTRA, HDIM - 2 * EXTRA), cols] = zeros

    def return_y(dz, to):
        return remote(
            part_out.at[dz, to], part_in.at[dz, y], p_send.at[dz, to], p_recv.at[dz, y], device(z, to, core)
        )

    def work(dz, yk, own):
        marks = (kv[dz, yk, pl.ds(BLK, EXTRA), pl.ds(0, BLK)].astype(F32) == sixteen.astype(F32)).astype(F32)
        ones = (lax.broadcasted_iota(jnp.int32, (HDIM - EXTRA, BLK), 0) < 6).astype(F32)
        tail = jnp.concatenate([marks, ones], axis=0).T.astype(BF16)
        for h in range(2):
            keys = kv[dz, yk, pl.ds(0, BLK), pl.ds(h * HDIM, HDIM)]
            values = kv[dz, yk, pl.ds(0, BLK), pl.ds((2 + h) * HDIM, HDIM)]
            keys_t = keys.T
            keys_long = jnp.concatenate([keys, tail], axis=1)
            values_long = jnp.concatenate([values, tail], axis=1)
            dk = jnp.zeros((BLK, HDIM), F32)
            dv = jnp.zeros((BLK, HDIM), F32)
            for c in range(ROWS // QC):
                cols = pl.ds(c * QC, QC)
                heads = [h * GROUP + c * (QC // BLK) + i for i in range(QC // BLK)]
                q_rows = jnp.concatenate([q_buf[:, pl.ds(n * HDIM, HDIM)] for n in heads], axis=0)
                g_rows = jnp.concatenate([g_buf[:, pl.ds(n * HDIM, HDIM)] for n in heads], axis=0)
                prob = jnp.exp2(dot(keys_long, qt[h, :, cols]) * EXP_SCALE)
                if own:
                    k_pos = lax.broadcasted_iota(jnp.int32, (BLK, QC), 0)
                    q_pos = lax.broadcasted_iota(jnp.int32, (BLK, QC), 1) % BLK
                    prob = jnp.where(k_pos <= q_pos, prob, 0.0)
                grad = prob * dot(values_long, gt[h, :, cols])
                prob_half = prob.astype(BF16)
                grad_half = grad.astype(BF16)
                dv = dv + dot(prob_half, g_rows)
                dk = dk + dot(grad_half, q_rows)
                if own:
                    dqt[h, :, cols] = dot(keys_t, grad_half)
                else:
                    dqt[h, :, cols] += dot(keys_t, grad_half)
            dk_lanes, dv_lanes = pl.ds(h * HDIM, HDIM), pl.ds((2 + h) * HDIM, HDIM)
            if own:
                acc[0, :, dk_lanes] = dk
                acc[0, :, dv_lanes] = dv
            else:

                @pl.when(yk == y)
                def _():
                    acc[dz, :, dk_lanes] = dk
                    acc[dz, :, dv_lanes] = dv

                @pl.when(yk != y)
                def _():
                    part_out[dz, yk, :, dk_lanes] = dk.astype(BF16)
                    part_out[dz, yk, :, dv_lanes] = dv.astype(BF16)

    work(0, y, True)

    @pl.loop(1, 4)
    def _(turn):
        dz = turn % 3
        first = (2 - dz) // 2 * (4 - y)
        last = 4 - dz // 2 * y
        live = (z - dz + 4) // 4

        @pl.loop(first, first + live * (last - first))
        def _(i):
            yk = (y + i) % 4
            pl.when((dz != 2) | (i != 0))(lambda: arrived(dz, yk))

            @pl.when((dz == 1) & (i == 0))
            def _():
                pl.when(z < 3)(lambda: along_z(1).start())
                each_target(1, lambda to: along_y(1, to).start())

            work(dz, yk, False)

            @pl.when((dz == 1) & (i == 0) & (z > 1))
            def _():
                arrived(2, y)
                each_target(2, lambda to: along_y(2, to).start())

            pl.when(yk != y)(lambda: return_y(dz, yk).start())

    for head in range(HEADS):
        h, cols = head // GROUP, pl.ds(head % GROUP * BLK, BLK)
        dq_half[:, pl.ds(head * HDIM, HDIM)] = (dqt[h, :, cols].T * SCALE).astype(BF16)
    mine = pl.ds(pl.multiple_of(core * TOK, TOK), TOK)
    theirs = pl.ds(pl.multiple_of(other * TOK, TOK), TOK)
    wide = pl.ds(pl.multiple_of(core * HEADS * HDIM, HEADS * HDIM), HEADS * HDIM)
    narrow = pl.ds(pl.multiple_of(core * 2 * HDIM, 2 * HDIM), 2 * HDIM)
    results = (
        (lambda rows: dq_half.at[rows], lambda: dq_out.at[:, wide]),
        (lambda rows: fin.at[rows, pl.ds(0, 2 * HDIM)], lambda: dk_out.at[:, narrow]),
        (lambda rows: fin.at[rows, pl.ds(2 * HDIM, 2 * HDIM)], lambda: dv_out.at[:, narrow]),
    )

    def keep(i):
        return pltpu.make_async_copy(results[i][0](mine), results[i][1](), f_local.at[i])

    def give(i):
        return remote(results[i][0](theirs), results[i][1](), f_send.at[i], f_recv.at[i], sibling)

    keep(0).start()
    give(0).start()

    def take(dz, yk):
        remote(
            part_out.at[dz, yk], part_in.at[dz, yk], p_send.at[dz, yk], p_recv.at[dz, yk], sibling
        ).wait_recv()
        acc[dz] += part_in[dz, yk].astype(F32)

    def each_source(dz, act):
        each_target(dz, act)

    def piece(dz, c):
        rows = pl.ds(c * CH, CH)
        return remote(acc.at[dz, rows], zin.at[2 - dz, rows], z_send.at[2 - dz, c], z_recv.at[2 - dz, c], down)

    def join(dz, c):
        rows = pl.ds(c * CH, CH)
        remote(acc.at[dz, rows], zin.at[1 - dz, rows], z_send.at[1 - dz, c], z_recv.at[1 - dz, c], sibling).wait_recv()
        acc[dz, rows] += zin[1 - dz, rows]

    @pl.when(z > 1)
    def _():
        each_source(2, lambda yk: take(2, yk))
        for c in range(NCH):
            piece(2, c).start()

    @pl.when(z > 0)
    def _():
        each_source(1, lambda yk: take(1, yk))
        for c in range(NCH):
            pl.when(z < 3)(lambda: join(1, c))
            piece(1, c).start()

    each_source(0, lambda yk: take(0, yk))
    for c in range(NCH):
        rows = pl.ds(c * CH, CH)
        pl.when(z < 3)(lambda: join(0, c))
        fin[rows, pl.ds(0, 2 * HDIM)] = (acc[0, rows, pl.ds(0, 2 * HDIM)] * SCALE).astype(BF16)
        fin[rows, pl.ds(2 * HDIM, 2 * HDIM)] = acc[0, rows, pl.ds(2 * HDIM, 2 * HDIM)].astype(BF16)
    for i in (1, 2):
        keep(i).start()
        give(i).start()

    for name in ITEMS:
        swap(name).wait_send()
    pl.when(z < 3)(lambda: along_z(0).wait_send())
    pl.when((z > 0) & (z < 3))(lambda: along_z(1).wait_send())
    each_target(0, lambda to: along_y(0, to).wait_send())
    pl.when(z > 0)(lambda: each_target(1, lambda to: along_y(1, to).wait_send()))
    pl.when(z > 1)(lambda: each_target(2, lambda to: along_y(2, to).wait_send()))
    for apart in range(1, 4):
        to = (y + apart) % 4
        pl.when(to < y)(lambda: return_y(0, to).wait_send())
        pl.when(z > 0)(lambda: return_y(1, to).wait_send())
        pl.when((z > 1) & (to > y))(lambda: return_y(2, to).wait_send())
    for c in range(NCH):
        pl.when(z > 1)(lambda: piece(2, c).wait_send())
        pl.when(z > 0)(lambda: piece(1, c).wait_send())
    for i in range(3):
        keep(i).wait()
        give(i).wait()


def on_device(queries, key_rows, value_rows, out_grad, log_norm, row_delta, doc_ids):
    dma = pltpu.SemaphoreType.DMA
    items = len(ITEMS)
    dq, dk, dv = pl.pallas_call(
        kernel,
        out_shape=(
            jax.ShapeDtypeStruct((TOK, 2 * HEADS * HDIM), BF16),
            jax.ShapeDtypeStruct((TOK, 4 * HDIM), BF16),
            jax.ShapeDtypeStruct((TOK, 4 * HDIM), BF16),
        ),
        in_specs=[pl.BlockSpec(memory_space=pl.ANY)] * 7,
        out_specs=[pl.BlockSpec(memory_space=pl.ANY)] * 3,
        scratch_shapes=[
            pltpu.VMEM((3, 4, BLK + EXTRA, 4 * HDIM), BF16),
            pltpu.VMEM((3, 4, BLK, 4 * HDIM), BF16),
            pltpu.VMEM((3, 4, BLK, 4 * HDIM), BF16),
            pltpu.VMEM((3, BLK, 4 * HDIM), F32),
            pltpu.VMEM((2, BLK, 4 * HDIM), F32),
            pltpu.VMEM((BLK, HEADS * HDIM), BF16),
            pltpu.VMEM((BLK, HEADS * HDIM), BF16),
            pltpu.VMEM((2, 2 * HDIM, ROWS), BF16),
            pltpu.VMEM((2, 2 * HDIM, ROWS), BF16),
            pltpu.VMEM((2, HDIM, ROWS), F32),
            pltpu.VMEM((BLK, HEADS * HDIM), BF16),
            pltpu.VMEM((BLK, 4 * HDIM), BF16),
            pltpu.VMEM((BLK, 2 * HEADS), F32),
            pltpu.VMEM((BLK, 2 * HEADS), F32),
            pltpu.VMEM((2, 1, TOK), jnp.int32),
            dma((items,)),
            dma((items,)),
            dma((items,)),
            dma((3, 4)),
            dma((3, 4)),
            dma((2,)),
            dma((3, 4)),
            dma((3, 4)),
            dma((2, NCH)),
            dma((2, NCH)),
            dma((3,)),
            dma((3,)),
            dma((3,)),
        ],
        compiler_params=pltpu.CompilerParams(
            collective_id=0, has_side_effects=True, vmem_limit_bytes=48 * 2**20
        ),
        name="attention_backward",
    )(queries[0], key_rows[0], value_rows[0], out_grad[0], log_norm[0], row_delta[0], doc_ids)
    return dq[None], dk[None], dv[None]


def solution(mesh):
    return jax.shard_map(
        on_device,
        mesh=mesh,
        in_specs=(P("dp", "seq", None),) * 6 + (P("dp", "seq"),),
        out_specs=(P("dp", "seq", None),) * 3,
        check_vma=False,
    )
```

time: 892 us -> 94.8 us (0.11)
  the two profiles are of different devices: /device:TPU:28 before, /device:TPU:189 now
where the time goes in v1:
time: 94.8 us; the launch traced here: 94.5 us
  Pallas kernels  85.9 us (91%)
  local copies, waits for them, and re-layouts  7.95 us (8%)
    pallas_call x1, Pallas kernels, on_device(): pl.pallas_call(kernel, out_shape=(jax.ShapeDtypeStruct((TOK, 2 * HEADS *...  85.9 us
    unnamed x15, local copies, waits for them, and re-layouts  7.95 us

profile of v1, /device:TPU:189, one launch (start us, length us, event | category | flops | bytes accessed | tf_op | source)
XLA Modules:
  0.0 94.5 jit_solution(864021907414494733)
XLA Ops:
  0.6 0.0 copy-start.2
  0.6 0.8 copy.10
  1.5 0.8 copy.11
  2.3 0.0 copy-start.4
  2.3 0.0 copy-done.2
  2.3 0.6 copy-done.4
  3.0 0.0 copy-start
  3.0 1.2 %copy-done = bf16[1,128,4096]{2,1,0:T(8,128)(2,1)S(1)} copy-done((bf16[1,128,4096]{2,1,0:T(8,128)(2,1)S(1)}, bf16[1,128,4096]{2,1,0:T(8,128)(2,1)}, u32[]{:S(2)}) %copy-start) | copy-done | bytes 1048600
  4.2 0.0 copy-start.1
  4.2 1.2 %copy-done.1 = bf16[1,128,4096]{2,1,0:T(8,128)(2,1)S(1)} copy-done((bf16[1,128,4096]{2,1,0:T(8,128)(2,1)S(1)}, bf16[1,128,4096]{2,1,0:T(8,128)(2,1)}, u32[]{:S(2)}) %copy-start.1) | copy-done | bytes 1048600
  5.4 0.0 copy-start.3
  5.4 0.9 copy-done.3
  6.3 85.9 %attention_backward.1 = (bf16[128,4096]{1,0:T(8,128)(2,1)S(1)}, bf16[128,512]{1,0:T(8,128)(2,1)S(1)}, bf16[128,512]{1,0:T(8,128)(2,1)S(1)}) custom-call(bf16[128,4096]{1,0:T(8,128)(2,1)S(1)} %bitcast.9, bf16[128,512]{1,0:T(8,128)(2,1)S(1)} %bitcast.16, bf16[128,512]{1,0:T(8,128)(2,1)S(1)} %bitcast.17, bf16[128,4096]{1,0:T(8,128)(2,1)S(1)} %bitcast.10, ...), custom_call_target="tpu_custom_call" | custom-call | tf_op jit(solution)/shard_map/attention_backward/pallas_call | solution.py:330
  92.2 1.0 %copy.15 = bf16[1,128,4096]{2,1,0:T(8,128)(2,1)} copy(bf16[1,128,4096]{2,1,0:T(8,128)(2,1)S(1)} %bitcast.11) | data formatting | bytes 2097152
  93.2 0.7 copy.16
  93.8 0.7 copy.17
Async XLA Ops:
  0.6 1.7 %copy-start.2 = (bf16[1,128,512]{2,1,0:T(8,128)(2,1)S(1)}, bf16[1,128,512]{2,1,0:T(8,128)(2,1)}, u32[]{:S(2)}) copy-start(bf16[1,128,512]{2,1,0:T(8,128)(2,1)} %param.8) | copy-start | bytes 393220
  2.3 0.7 copy-start.4
  3.0 1.2 %copy-start = (bf16[1,128,4096]{2,1,0:T(8,128)(2,1)S(1)}, bf16[1,128,4096]{2,1,0:T(8,128)(2,1)}, u32[]{:S(2)}) copy-start(bf16[1,128,4096]{2,1,0:T(8,128)(2,1)} %param.7) | copy-start | bytes 3145732
  4.2 1.2 %copy-start.1 = (bf16[1,128,4096]{2,1,0:T(8,128)(2,1)S(1)}, bf16[1,128,4096]{2,1,0:T(8,128)(2,1)}, u32[]{:S(2)}) copy-start(bf16[1,128,4096]{2,1,0:T(8,128)(2,1)} %param.10) | copy-start | bytes 3145732
  5.4 0.9 copy-start.3

commit v2 on v0

v2 whole, which is shorter than its diff:
```python
import jax
import jax.numpy as jnp
from jax import lax
from jax.experimental import pallas as pl
from jax.experimental.pallas import tpu as pltpu
from jax.sharding import PartitionSpec as P

F32, BF16 = jnp.float32, jnp.bfloat16
HDIM = 128
TOK = 128
BLK = 2 * TOK
HEADS = 4
GROUP = 8
WIDE = HEADS * HDIM
COLS = HEADS * BLK
QC = 1024
SCALE = HDIM**-0.5
EXP_SCALE = SCALE * 1.4426950408889634
FAR = -1e30
MARKS = 16
KINDS = ("q", "g", "lse", "delta", "doc")
SUMS = BF16


def dot(a, b):
    return jnp.dot(a, b, preferred_element_type=F32)


def split3(x):
    hi = x.astype(BF16).astype(F32)
    mid = (x - hi).astype(BF16).astype(F32)
    return hi, mid, x - hi - mid


def kernel(
    q_in, k_in, v_in, g_in, lse_in, delta_in, doc_in,
    dq_out, dk_out, dv_out,
    q_buf, g_buf, lse_buf, delta_buf, doc_buf, kv, qt, gt, dqt, tails, keys_t, acc, xin, zout, zin, dq_half, fin,
    x_local, x_send, x_recv, kv_local, kv_send, kv_recv, half_send, half_recv, kvz_send, kvz_recv, docz_send, docz_recv,
    s_send, s_recv, z_send, z_recv, dq_local, dq_send, dq_recv, f_local, f_send, f_recv,
):
    me = lax.axis_index("seq")
    core = me % 2
    other = 1 - core
    y = (me // 2) % 4
    z = me // 8
    here = me % 8

    def remote(src, dst, send, recv, to):
        return pltpu.make_async_remote_copy(
            src_ref=src, dst_ref=dst, send_sem=send, recv_sem=recv,
            device_id={"seq": to}, device_id_type=pl.DeviceIdType.MESH,
        )

    row = z * 8
    sibling = row + y * 2 + other
    down, up = me - 8, me + 8

    def lanes(i, size):
        return pl.ds(pl.multiple_of(i * size, size), size)

    def source(kind, p):
        return {
            "q": lambda: q_in.at[:, lanes(p, WIDE)],
            "g": lambda: g_in.at[:, lanes(p, WIDE)],
            "lse": lambda: lse_in.at[lanes(p // 2, GROUP)],
            "delta": lambda: delta_in.at[lanes(p // 2, GROUP)],
            "doc": lambda: doc_in,
        }[kind]()

    def target(kind, p):
        return {
            "q": lambda: q_buf.at[p],
            "g": lambda: g_buf.at[p],
            "lse": lambda: lse_buf.at[p],
            "delta": lambda: delta_buf.at[p],
            "doc": lambda: doc_buf.at[0, p],
        }[kind]()

    def stay(kind):
        return pltpu.make_async_copy(source(kind, here), target(kind, here), x_local.at[KINDS.index(kind)])

    def send(kind, p):
        i = KINDS.index(kind)
        return remote(source(kind, p), target(kind, here), x_send.at[i, p], x_recv.at[i, here], row + p)

    def receive(kind, p):
        i = KINDS.index(kind)
        remote(source(kind, p), target(kind, p), x_send.at[i, p], x_recv.at[i, p], sibling).wait_recv()

    def kv_place(part, column):
        return kv.at[0, core, column, :, pl.ds(part * HDIM, HDIM)]

    def kv_source(part, column):
        return (k_in, v_in)[part].at[:, lanes(column, HDIM)]

    def kv_stay(part):
        return pltpu.make_async_copy(kv_source(part, y), kv_place(part, y), kv_local.at[part])

    def kv_give(part, column):
        return remote(
            kv_source(part, column), kv_place(part, y), kv_send.at[part, column], kv_recv.at[part, y],
            row + column * 2 + core,
        )

    def kv_take(part, column):
        remote(
            kv_source(part, column), kv_place(part, column), kv_send.at[part, column], kv_recv.at[part, column], sibling
        ).wait_recv()

    for part in range(2):
        kv_stay(part).start()
    for kind in KINDS:
        stay(kind).start()

    barrier = pltpu.get_barrier_semaphore()

    def greet(to):
        pl.semaphore_signal(barrier, inc=1, device_id={"seq": to}, device_id_type=pl.DeviceIdType.MESH)

    for apart in range(1, 8):
        greet(row + (here + apart) % 8)
    pl.when(z > 0)(lambda: greet(down))
    pl.when(z < 3)(lambda: greet(up))
    pl.semaphore_wait(barrier, 7 + (z + 3) // 4 + (6 - z) // 4)

    columns = [(y + apart) % 4 for apart in (1, 3, 2)]
    others = [sibling - row] + [column * 2 + c for column in columns for c in range(2)]
    for column in columns:
        for part in range(2):
            kv_give(part, column).start()
    for p in others:
        send("doc", p).start()
    for kind in ("q", "g", "lse", "delta"):
        send(kind, others[0]).start()

    def half(dz):
        return remote(kv.at[dz, core], kv.at[dz, core], half_send.at[dz], half_recv.at[dz], sibling)

    def half_take(dz):
        remote(kv.at[dz, other], kv.at[dz, other], half_send.at[dz], half_recv.at[dz], sibling).wait_recv()

    def kv_up(dz):
        return remote(kv.at[dz, core], kv.at[dz + 1, core], kvz_send.at[dz], kvz_recv.at[dz], up)

    def doc_up(dz):
        return remote(doc_buf.at[dz], doc_buf.at[dz + 1], docz_send.at[dz], docz_recv.at[dz], up)

    for part in range(2):
        kv_stay(part).wait()
        for column in columns:
            kv_take(part, column)
    half(0).start()
    pl.when(z < 3)(lambda: kv_up(0).start())
    for p in others[1:5]:
        for kind in ("q", "g", "lse", "delta"):
            send(kind, p).start()
    stay("doc").wait()
    for p in others:
        receive("doc", p)
    pl.when(z < 3)(lambda: doc_up(0).start())
    acc[...] = jnp.zeros_like(acc)
    half_take(0)

    sixteen = lax.broadcasted_iota(jnp.int32, (MARKS, BLK), 0).astype(F32)

    def marks_of(dz, column):
        docs = jnp.concatenate([doc_buf[dz, column * 2], doc_buf[dz, column * 2 + 1]], axis=1).astype(F32)
        return jnp.broadcast_to(docs, (MARKS, BLK)) == sixteen

    def prepare_keys(dz):
        @pl.loop(0, 4)
        def _(column):
            marks = marks_of(dz, column).astype(F32)
            ones = (lax.broadcasted_iota(jnp.int32, (HDIM - MARKS, BLK), 0) < 6).astype(F32)
            tails[dz, column] = jnp.concatenate([marks, ones], axis=0).T.astype(BF16)
            keys_t[dz, column] = both(kv, dz, column, 0).T

    def both(ref, dz, column, part):
        at = pl.ds(part * HDIM, HDIM)
        return jnp.concatenate([ref[dz, 0, column, :, at], ref[dz, 1, column, :, at]], axis=0)

    def rows_of(buf, column, head):
        at = pl.ds(head * HDIM, HDIM)
        return jnp.concatenate([buf[column * 2, :, at], buf[column * 2 + 1, :, at]], axis=0)

    def prepare_queries(column):
        bias = jnp.where(marks_of(0, column), 0.0, FAR).astype(BF16)
        blank = jnp.zeros((MARKS, BLK), BF16)
        zeros = jnp.zeros((HDIM - 2 * MARKS, BLK), BF16)

        def statistic(buf, factor):
            pair = [buf[column * 2], buf[column * 2 + 1]]
            pair = [jnp.where(core == 0, rows[:HEADS], rows[HEADS:]) for rows in pair]
            return split3(jnp.concatenate(pair, axis=1) * factor)

        for buf, out, first, top, parts in (
            (q_buf, qt, 0, bias, statistic(lse_buf, -1.0 / SCALE)), (g_buf, gt, 3, blank, statistic(delta_buf, -1.0))
        ):
            for head in range(HEADS):
                at = pl.ds(head * BLK, BLK)
                rows = jnp.zeros((MARKS, BLK), F32)
                for i, part in enumerate(parts):
                    rows = jnp.where(sixteen == first + i, jnp.broadcast_to(part[head : head + 1], (MARKS, BLK)), rows)
                out[column, pl.ds(0, HDIM), at] = rows_of(buf, column, head).T
                out[column, pl.ds(HDIM, MARKS), at] = top
                out[column, pl.ds(HDIM + MARKS, MARKS), at] = rows.astype(BF16)
                out[column, pl.ds(HDIM + 2 * MARKS, HDIM - 2 * MARKS), at] = zeros
        dqt[column] = jnp.zeros((HDIM, COLS), F32)

    def work(dz, yk, yq, own):
        tail = tails[dz, yk]
        keys_long = jnp.concatenate([both(kv, dz, yk, 0), tail], axis=1)
        values_long = jnp.concatenate([both(kv, dz, yk, 1), tail], axis=1)
        dk = jnp.zeros((BLK, HDIM), F32)
        dv = jnp.zeros((BLK, HDIM), F32)
        for c in range(COLS // QC):
            cols = pl.ds(c * QC, QC)
            heads = [c * (QC // BLK) + i for i in range(QC // BLK)]
            q_rows = jnp.concatenate([rows_of(q_buf, yq, n) for n in heads], axis=0)
            g_rows = jnp.concatenate([rows_of(g_buf, yq, n) for n in heads], axis=0)
            prob = jnp.exp2(dot(keys_long, qt[yq, :, cols]) * EXP_SCALE)
            if own:
                k_pos = lax.broadcasted_iota(jnp.int32, (BLK, QC), 0)
                q_pos = lax.broadcasted_iota(jnp.int32, (BLK, QC), 1) % BLK
                prob = jnp.where(k_pos <= q_pos, prob, 0.0)
            grad = prob * dot(values_long, gt[yq, :, cols])
            prob_half = prob.astype(BF16)
            grad_half = grad.astype(BF16)
            dv = dv + dot(prob_half, g_rows)
            dk = dk + dot(grad_half, q_rows)
            dqt[yq, :, cols] += dot(keys_t[dz, yk], grad_half)
        for c in range(2):
            acc[dz, c, yk, :, pl.ds(0, HDIM)] += dk[c * TOK : (c + 1) * TOK]
            acc[dz, c, yk, :, pl.ds(HDIM, HDIM)] += dv[c * TOK : (c + 1) * TOK]

    def dq_keep():
        return pltpu.make_async_copy(dq_half.at[y, core], dq_out.at[:, lanes(here, WIDE)], dq_local)

    def dq_give(column, c):
        return remote(
            dq_half.at[column, c], dq_out.at[:, lanes(here, WIDE)], dq_send.at[column, c], dq_recv.at[here],
            row + column * 2 + c,
        )

    def dq_take(p):
        remote(
            dq_half.at[0, 0], dq_out.at[:, lanes(p, WIDE)], dq_send.at[0, 0], dq_recv.at[p], sibling
        ).wait_recv()

    def finish_queries(column):
        for head in range(HEADS):
            done = (dqt[column, :, pl.ds(head * BLK, BLK)].T * SCALE).astype(BF16)
            for c in range(2):
                dq_half[column, c, :, pl.ds(head * HDIM, HDIM)] = done[c * TOK : (c + 1) * TOK]

        @pl.when(column == y)
        def _():
            dq_keep().start()
            dq_give(y, other).start()

        @pl.when(column != y)
        def _():
            for c in range(2):
                dq_give(column, c).start()

    def share(dz):
        return remote(acc.at[dz, other], xin.at[dz], s_send.at[dz], s_recv.at[dz], sibling)

    def along(dz):
        return remote(zout.at[2 - dz], zin.at[2 - dz], z_send.at[2 - dz], z_recv.at[2 - dz], down)

    def join(dz):
        share(dz).wait_recv()
        total = acc[dz, core] + xin[dz]
        acc[dz, core] = total

    def join_above(dz):
        remote(zout.at[1 - dz], zin.at[1 - dz], z_send.at[1 - dz], z_recv.at[1 - dz], down).wait_recv()
        acc[dz, core] += zin[1 - dz].astype(F32)

    def pass_down(dz):
        zout[2 - dz] = acc[dz, core].astype(SUMS)
        along(dz).start()

    @pl.loop(0, 12)
    def _(s):
        from1, from4, from8, from9, from10 = ((s + 12 - n) // 12 for n in (1, 4, 8, 9, 10))
        dz = from1 + from4 - from8 - from9
        turn = from1 * (s - 1) - 3 * from4 - from8 - from9 - 3 * from10
        yq = (y + turn + turn // 2 - 2 * (turn // 3)) % 4
        is0, is2 = (2 - dz) // 2, dz // 2
        live = (z - dz + 4) // 4
        first = is2 * yq
        last = 4 - is0 * (3 - yq)

        @pl.when((s == 1) & (z > 0))
        def _():
            kv_up(0).wait_recv()
            half(1).start()
            pl.when(z < 3)(lambda: kv_up(1).start())
            doc_up(0).wait_recv()
            pl.when(z < 3)(lambda: doc_up(1).start())
            half_take(1)

        @pl.when((s == 3) & (z > 1))
        def _():
            kv_up(1).wait_recv()
            half(2).start()
            doc_up(1).wait_recv()

        @pl.when((s == 4) & (z > 1))
        def _():
            half_take(2)

        pl.when(((s < 2) | (s == 4)) & (z >= dz))(lambda: prepare_keys(dz))

        @pl.when((s == 0) | (s == 2) | (s == 3) | (s == 7))
        def _():
            @pl.when(s == 0)
            def _():
                for kind in ("q", "g", "lse", "delta"):
                    stay(kind).wait()
                    receive(kind, others[0])

            @pl.when(s != 0)
            def _():
                for kind in ("q", "g", "lse", "delta"):
                    for c in range(2):
                        receive(kind, yq * 2 + c)

            @pl.when(s == 2)
            def _():
                for p in others[5:]:
                    for kind in ("q", "g", "lse", "delta"):
                        send(kind, p).start()

            prepare_queries(yq)

        @pl.loop(first, first + live * (last - first))
        def _(yk):
            diagonal = (dz == 0) & (yk == yq)
            pl.when(diagonal)(lambda: work(0, yq, yq, True))
            pl.when(jnp.logical_not(diagonal))(lambda: work(dz, yk, yq, False))

        @pl.when((s == 4) | (s >= 9))
        def _():
            finish_queries(yq)

        @pl.when((s == 7) & (z > 1))
        def _():
            share(2).start()

        @pl.when((s == 8) & (z > 0))
        def _():
            share(1).start()

            @pl.when(z > 1)
            def _():
                join(2)
                pass_down(2)

    share(0).start()

    @pl.when(z > 0)
    def _():
        join(1)
        pl.when(z < 3)(lambda: join_above(1))
        pass_down(1)

    join(0)
    pl.when(z < 3)(lambda: join_above(0))
    for column in range(4):
        fin[column, :, pl.ds(0, HDIM)] = (acc[0, core, column, :, pl.ds(0, HDIM)] * SCALE).astype(BF16)
        fin[column, :, pl.ds(HDIM, HDIM)] = acc[0, core, column, :, pl.ds(HDIM, HDIM)].astype(BF16)

    def fin_keep(part):
        return pltpu.make_async_copy(
            fin.at[y, :, pl.ds(part * HDIM, HDIM)], (dk_out, dv_out)[part].at[:, lanes(y, HDIM)], f_local.at[part]
        )

    def fin_give(part, column):
        return remote(
            fin.at[column, :, pl.ds(part * HDIM, HDIM)], (dk_out, dv_out)[part].at[:, lanes(y, HDIM)],
            f_send.at[part, column], f_recv.at[part, y], row + column * 2 + core,
        )

    def fin_take(part, column):
        remote(
            fin.at[column, :, pl.ds(part * HDIM, HDIM)], (dk_out, dv_out)[part].at[:, lanes(column, HDIM)],
            f_send.at[part, column], f_recv.at[part, column], sibling,
        ).wait_recv()

    for part in range(2):
        for column in columns:
            fin_give(part, column).start()
        fin_keep(part).start()

    for p in others:
        for kind in KINDS:
            send(kind, p).wait_send()
        dq_take(p)
    for dz in range(3):
        pl.when(z >= dz)(lambda dz=dz: half(dz).wait_send())
        pl.when(z >= dz)(lambda dz=dz: share(dz).wait_send())
    for dz in range(2):

        @pl.when((z >= dz) & (z < 3))
        def _():
            kv_up(dz).wait_send()
            doc_up(dz).wait_send()

    for dz in (1, 2):
        pl.when(z >= dz)(lambda dz=dz: along(dz).wait_send())
    dq_keep().wait()
    dq_give(y, other).wait_send()
    for column in columns:
        for c in range(2):
            dq_give(column, c).wait_send()
        for part in range(2):
            kv_give(part, column).wait_send()
            fin_give(part, column).wait_send()
            fin_take(part, column)
    for part in range(2):
        fin_keep(part).wait()


def on_device(queries, key_rows, value_rows, out_grad, log_norm, row_delta, doc_ids):
    dma = pltpu.SemaphoreType.DMA
    kinds = len(KINDS)
    dq, dk, dv = pl.pallas_call(
        kernel,
        out_shape=(
            jax.ShapeDtypeStruct((TOK, 8 * WIDE), BF16),
            jax.ShapeDtypeStruct((TOK, 4 * HDIM), BF16),
            jax.ShapeDtypeStruct((TOK, 4 * HDIM), BF16),
        ),
        in_specs=[pl.BlockSpec(memory_space=pl.ANY)] * 7,
        out_specs=[pl.BlockSpec(memory_space=pl.ANY)] * 3,
        scratch_shapes=[
            pltpu.VMEM((8, TOK, WIDE), BF16),
            pltpu.VMEM((8, TOK, WIDE), BF16),
            pltpu.VMEM((8, GROUP, TOK), F32),
            pltpu.VMEM((8, GROUP, TOK), F32),
            pltpu.VMEM((3, 8, 1, TOK), jnp.int32),
            pltpu.VMEM((3, 2, 4, TOK, 2 * HDIM), BF16),
            pltpu.VMEM((4, 2 * HDIM, COLS), BF16),
            pltpu.VMEM((4, 2 * HDIM, COLS), BF16),
            pltpu.VMEM((4, HDIM, COLS), F32),
            pltpu.VMEM((3, 4, BLK, HDIM), BF16),
            pltpu.VMEM((3, 4, HDIM, BLK), BF16),
            pltpu.VMEM((3, 2, 4, TOK, 2 * HDIM), F32),
            pltpu.VMEM((3, 4, TOK, 2 * HDIM), F32),
            pltpu.VMEM((2, 4, TOK, 2 * HDIM), SUMS),
            pltpu.VMEM((2, 4, TOK, 2 * HDIM), SUMS),
            pltpu.VMEM((4, 2, TOK, WIDE), BF16),
            pltpu.VMEM((4, TOK, 2 * HDIM), BF16),
            dma((kinds,)),
            dma((kinds, 8)),
            dma((kinds, 8)),
            dma((2,)),
            dma((2, 4)),
            dma((2, 4)),
            dma((3,)),
            dma((3,)),
            dma((2,)),
            dma((2,)),
            dma((2,)),
            dma((2,)),
            dma((3,)),
            dma((3,)),
            dma((2,)),
            dma((2,)),
            dma,
            dma((4, 2)),
            dma((8,)),
            dma((2,)),
            dma((2, 4)),
            dma((2, 4)),
        ],
        compiler_params=pltpu.CompilerParams(
            collective_id=0, has_side_effects=True, vmem_limit_bytes=60 * 2**20
        ),
        name="attention_backward",
    )(queries[0], key_rows[0], value_rows[0], out_grad[0], log_norm[0].T, row_delta[0].T, doc_ids)
    return dq[None], dk[None], dv[None]


def solution(mesh):
    return jax.shard_map(
        on_device,
        mesh=mesh,
        in_specs=(P("dp", "seq", None),) * 6 + (P("dp", "seq"),),
        out_specs=(P("dp", "seq", None),) * 3,
        check_vma=False,
    )
```

time: 892 us -> 70.7 us (0.08)
  the two profiles are of different devices: /device:TPU:28 before, /device:TPU:1 now
where the time goes in v2:
time: 70.7 us; the launch traced here: 70.5 us
  Pallas kernels  65.9 us (93%)
  local copies, waits for them, and re-layouts  3.93 us (6%)
    pallas_call x1, Pallas kernels, on_device(): pl.pallas_call(kernel, out_shape=(jax.ShapeDtypeStruct((TOK, 8 * WIDE), B...  65.9 us
    unnamed x7, local copies, waits for them, and re-layouts  3.93 us

profile of v2, /device:TPU:1, one launch (start us, length us, event | category | flops | bytes accessed | tf_op | source)
XLA Modules:
  0.0 70.5 jit_solution(17771866427672025668)
XLA Ops:
  0.6 65.9 %attention_backward.1 = (bf16[128,4096]{1,0:T(8,128)(2,1)}, bf16[128,512]{1,0:T(8,128)(2,1)}, bf16[128,512]{1,0:T(8,128)(2,1)}) custom-call(bf16[128,4096]{1,0:T(8,128)(2,1)} %bitcast.14, bf16[128,512]{1,0:T(8,128)(2,1)} %bitcast.18, bf16[128,512]{1,0:T(8,128)(2,1)} %bitcast.19, bf16[128,4096]{1,0:T(8,128)(2,1)} %bitcast.15, f32[32,128]{1,0:T(8,128)} %bitcast.20, ...), custom_call_target="tpu_custom_call" | custom-call | tf_op jit(solution)/shard_map/attention_backward/pallas_call | solution.py:431
  66.6 0.0 copy-start.1
  66.6 2.3 %copy.13 = bf16[1,128,4096]{2,1,0:T(8,128)(2,1)} copy(bf16[1,128,4096]{2,1,0:T(8,128)(2,1)} %bitcast.13) | data formatting | bytes 2097152
  68.9 0.0 copy-done.1
  68.9 0.0 copy-start
  68.9 0.7 copy.14
  69.6 0.3 copy-done
  69.9 0.7 copy.15
Async XLA Ops:
  66.6 2.3 %copy-start.1 = (bf16[128,512]{1,0:T(8,128)(2,1)S(1)}, bf16[128,512]{1,0:T(8,128)(2,1)}, u32[]{:S(2)}) copy-start(bf16[128,512]{1,0:T(8,128)(2,1)} %get-tuple-element.7) | copy-start | bytes 393220
  68.9 1.0 %copy-start = (bf16[128,512]{1,0:T(8,128)(2,1)S(1)}, bf16[128,512]{1,0:T(8,128)(2,1)}, u32[]{:S(2)}) copy-start(bf16[128,512]{1,0:T(8,128)(2,1)} %get-tuple-element.8) | copy-start | bytes 393220

commit v3 on v2

--- a/solution.py
+++ b/solution.py
@@ -113,6 +113,7 @@
     for kind in KINDS:
         stay(kind).start()
 
+    acc[...] = jnp.zeros_like(acc)
     barrier = pltpu.get_barrier_semaphore()
 
     def greet(to):
@@ -131,8 +132,9 @@
             kv_give(part, column).start()
     for p in others:
         send("doc", p).start()
-    for kind in ("q", "g", "lse", "delta"):
-        send(kind, others[0]).start()
+    for p in others[:5]:
+        for kind in ("q", "g", "lse", "delta"):
+            send(kind, p).start()
 
     def half(dz):
         return remote(kv.at[dz, core], kv.at[dz, core], half_send.at[dz], half_recv.at[dz], sibling)
@@ -140,26 +142,26 @@
     def half_take(dz):
         remote(kv.at[dz, other], kv.at[dz, other], half_send.at[dz], half_recv.at[dz], sibling).wait_recv()
 
-    def kv_up(dz):
-        return remote(kv.at[dz, core], kv.at[dz + 1, core], kvz_send.at[dz], kvz_recv.at[dz], up)
+    def kv_up(dz, column):
+        return remote(
+            kv.at[dz, core, column], kv.at[dz + 1, core, column], kvz_send.at[dz, column], kvz_recv.at[dz, column], up
+        )
 
     def doc_up(dz):
         return remote(doc_buf.at[dz], doc_buf.at[dz + 1], docz_send.at[dz], docz_recv.at[dz], up)
 
     for part in range(2):
         kv_stay(part).wait()
-        for column in columns:
+    pl.when(z < 3)(lambda: kv_up(0, y).start())
+    for column in columns:
+        for part in range(2):
             kv_take(part, column)
+        pl.when(z < 3)(lambda column=column: kv_up(0, column).start())
     half(0).start()
-    pl.when(z < 3)(lambda: kv_up(0).start())
-    for p in others[1:5]:
-        for kind in ("q", "g", "lse", "delta"):
-            send(kind, p).start()
     stay("doc").wait()
     for p in others:
         receive("doc", p)
     pl.when(z < 3)(lambda: doc_up(0).start())
-    acc[...] = jnp.zeros_like(acc)
     half_take(0)
 
     sixteen = lax.broadcasted_iota(jnp.int32, (MARKS, BLK), 0).astype(F32)
@@ -208,12 +210,17 @@
                 out[column, pl.ds(HDIM + 2 * MARKS, HDIM - 2 * MARKS), at] = zeros
         dqt[column] = jnp.zeros((HDIM, COLS), F32)
 
-    def work(dz, yk, yq, own):
-        tail = tails[dz, yk]
-        keys_long = jnp.concatenate([both(kv, dz, yk, 0), tail], axis=1)
-        values_long = jnp.concatenate([both(kv, dz, yk, 1), tail], axis=1)
-        dk = jnp.zeros((BLK, HDIM), F32)
-        dv = jnp.zeros((BLK, HDIM), F32)
+    def work(dz, yks, yq, own=False):
+        size = BLK * len(yks)
+
+        def long(part):
+            blocks = [jnp.concatenate([both(kv, dz, yk, part), tails[dz, yk]], axis=1) for yk in yks]
+            return jnp.concatenate(blocks, axis=0)
+
+        keys_long, values_long = long(0), long(1)
+        across = jnp.concatenate([keys_t[dz, yk] for yk in yks], axis=1)
+        dk = jnp.zeros((size, HDIM), F32)
+        dv = jnp.zeros((size, HDIM), F32)
         for c in range(COLS // QC):
             cols = pl.ds(c * QC, QC)
             heads = [c * (QC // BLK) + i for i in range(QC // BLK)]
@@ -229,10 +236,12 @@
             grad_half = grad.astype(BF16)
             dv = dv + dot(prob_half, g_rows)
             dk = dk + dot(grad_half, q_rows)
-            dqt[yq, :, cols] += dot(keys_t[dz, yk], grad_half)
-        for c in range(2):
-            acc[dz, c, yk, :, pl.ds(0, HDIM)] += dk[c * TOK : (c + 1) * TOK]
-            acc[dz, c, yk, :, pl.ds(HDIM, HDIM)] += dv[c * TOK : (c + 1) * TOK]
+            dqt[yq, :, cols] += dot(across, grad_half)
+        for i, yk in enumerate(yks):
+            for c in range(2):
+                at = slice(i * BLK + c * TOK, i * BLK + (c + 1) * TOK)
+                acc[dz, c, yk, :, pl.ds(0, HDIM)] += dk[at]
+                acc[dz, c, yk, :, pl.ds(HDIM, HDIM)] += dv[at]
 
     def dq_keep():
         return pltpu.make_async_copy(dq_half.at[y, core], dq_out.at[:, lanes(here, WIDE)], dq_local)
@@ -267,21 +276,24 @@
     def share(dz):
         return remote(acc.at[dz, other], xin.at[dz], s_send.at[dz], s_recv.at[dz], sibling)
 
-    def along(dz):
-        return remote(zout.at[2 - dz], zin.at[2 - dz], z_send.at[2 - dz], z_recv.at[2 - dz], down)
+    def along(dz, column):
+        i = 2 - dz
+        return remote(zout.at[i, column], zin.at[i, column], z_send.at[i, column], z_recv.at[i, column], down)
 
     def join(dz):
         share(dz).wait_recv()
-        total = acc[dz, core] + xin[dz]
-        acc[dz, core] = total
-
-    def join_above(dz):
-        remote(zout.at[1 - dz], zin.at[1 - dz], z_send.at[1 - dz], z_recv.at[1 - dz], down).wait_recv()
-        acc[dz, core] += zin[1 - dz].astype(F32)
-
-    def pass_down(dz):
-        zout[2 - dz] = acc[dz, core].astype(SUMS)
-        along(dz).start()
+        acc[dz, core] += xin[dz]
+
+    def join_above(dz, column):
+        i = 1 - dz
+        remote(
+            zout.at[i, column], zin.at[i, column], z_send.at[i, column], z_recv.at[i, column], down
+        ).wait_recv()
+        acc[dz, core, column] += zin[i, column].astype(F32)
+
+    def pass_down(dz, column):
+        zout[2 - dz, column] = acc[dz, core, column].astype(SUMS)
+        along(dz, column).start()
 
     @pl.loop(0, 12)
     def _(s):
@@ -290,22 +302,29 @@
         turn = from1 * (s - 1) - 3 * from4 - from8 - from9 - 3 * from10
         yq = (y + turn + turn // 2 - 2 * (turn // 3)) % 4
         is0, is2 = (2 - dz) // 2, dz // 2
-        live = (z - dz + 4) // 4
         first = is2 * yq
-        last = 4 - is0 * (3 - yq)
+        count = is0 * yq + is2 * (z // 2) * (4 - yq)
 
         @pl.when((s == 1) & (z > 0))
         def _():
-            kv_up(0).wait_recv()
+            for column in [y] + columns:
+                kv_up(0, column).wait_recv()
+                pl.when(z < 3)(lambda column=column: kv_up(1, column).start())
             half(1).start()
-            pl.when(z < 3)(lambda: kv_up(1).start())
             doc_up(0).wait_recv()
             pl.when(z < 3)(lambda: doc_up(1).start())
             half_take(1)
 
+        @pl.when(s == 2)
+        def _():
+            for p in others[5:]:
+                for kind in ("q", "g", "lse", "delta"):
+                    send(kind, p).start()
+
         @pl.when((s == 3) & (z > 1))
         def _():
-            kv_up(1).wait_recv()
+            for column in [y] + columns:
+                kv_up(1, column).wait_recv()
             half(2).start()
             doc_up(1).wait_recv()
 
@@ -329,23 +348,16 @@
                     for c in range(2):
                         receive(kind, yq * 2 + c)
 
-            @pl.when(s == 2)
-            def _():
-                for p in others[5:]:
-                    for kind in ("q", "g", "lse", "delta"):
-                        send(kind, p).start()
-
             prepare_queries(yq)
 
-        @pl.loop(first, first + live * (last - first))
-        def _(yk):
-            diagonal = (dz == 0) & (yk == yq)
-            pl.when(diagonal)(lambda: work(0, yq, yq, True))
-            pl.when(jnp.logical_not(diagonal))(lambda: work(dz, yk, yq, False))
-
-        @pl.when((s == 4) | (s >= 9))
-        def _():
-            finish_queries(yq)
+        pl.when(dz == 0)(lambda: work(0, [yq], yq, True))
+        pl.when((dz == 1) & (z > 0))(lambda: work(1, [0, 1, 2, 3], yq))
+
+        @pl.loop(0, count // 2)
+        def _(i):
+            work(dz, [first + 2 * i, first + 2 * i + 1], yq)
+
+        pl.when(count % 2 == 1)(lambda: work(dz, [first + count - 1], yq))
 
         @pl.when((s == 7) & (z > 1))
         def _():
@@ -358,21 +370,24 @@
             @pl.when(z > 1)
             def _():
                 join(2)
-                pass_down(2)
-
-    share(0).start()
-
-    @pl.when(z > 0)
-    def _():
-        join(1)
-        pl.when(z < 3)(lambda: join_above(1))
-        pass_down(1)
-
-    join(0)
-    pl.when(z < 3)(lambda: join_above(0))
-    for column in range(4):
-        fin[column, :, pl.ds(0, HDIM)] = (acc[0, core, column, :, pl.ds(0, HDIM)] * SCALE).astype(BF16)
-        fin[column, :, pl.ds(HDIM, HDIM)] = acc[0, core, column, :, pl.ds(HDIM, HDIM)].astype(BF16)
+                for column in range(4):
+                    pass_down(2, column)
+
+        pl.when((s == 9) & (z > 0))(lambda: join(1))
+
+        @pl.when((s == 10) & (z > 0))
+        def _():
+            @pl.loop(0, 4)
+            def _(column):
+                pl.when(z < 3)(lambda: join_above(1, column))
+                pass_down(1, column)
+
+        pl.when(s == 11)(lambda: share(0).start())
+
+        @pl.when((s == 4) | (s >= 9))
+        def _():
+            finish_queries(yq)
+
 
     def fin_keep(part):
         return pltpu.make_async_copy(
@@ -391,10 +406,23 @@
             f_send.at[part, column], f_recv.at[part, column], sibling,
         ).wait_recv()
 
-    for part in range(2):
-        for column in columns:
-            fin_give(part, column).start()
-        fin_keep(part).start()
+    join(0)
+
+    @pl.loop(0, 4)
+    def _(column):
+        pl.when(z < 3)(lambda: join_above(0, column))
+        fin[column, :, pl.ds(0, HDIM)] = (acc[0, core, column, :, pl.ds(0, HDIM)] * SCALE).astype(BF16)
+        fin[column, :, pl.ds(HDIM, HDIM)] = acc[0, core, column, :, pl.ds(HDIM, HDIM)].astype(BF16)
+
+        @pl.when(column != y)
+        def _():
+            for part in range(2):
+                fin_give(part, column).start()
+
+        @pl.when(column == y)
+        def _():
+            for part in range(2):
+                fin_keep(part).start()
 
     for p in others:
         for kind in KINDS:
@@ -407,11 +435,13 @@
 
         @pl.when((z >= dz) & (z < 3))
         def _():
-            kv_up(dz).wait_send()
+            for column in range(4):
+                kv_up(dz, column).wait_send()
             doc_up(dz).wait_send()
 
     for dz in (1, 2):
-        pl.when(z >= dz)(lambda dz=dz: along(dz).wait_send())
+        for column in range(4):
+            pl.when(z >= dz)(lambda dz=dz, column=column: along(dz, column).wait_send())
     dq_keep().wait()
     dq_give(y, other).wait_send()
     for column in columns:
@@ -463,14 +493,14 @@
             dma((2, 4)),
             dma((3,)),
             dma((3,)),
-            dma((2,)),
-            dma((2,)),
+            dma((2, 4)),
+            dma((2, 4)),
             dma((2,)),
             dma((2,)),
             dma((3,)),
             dma((3,)),
-            dma((2,)),
-            dma((2,)),
+            dma((2, 4)),
+            dma((2, 4)),
             dma,
             dma((4, 2)),
             dma((8,)),

time: 70.7 us -> 66.6 us (0.942)
  the two profiles are of different devices: /device:TPU:1 before, /device:TPU:48 now
where the time goes in v3:
time: 66.6 us; the launch traced here: 66.4 us
  Pallas kernels  61.8 us (93%)
  local copies, waits for them, and re-layouts  3.93 us (6%)
    pallas_call x1, Pallas kernels, on_device(): pl.pallas_call(kernel, out_shape=(jax.ShapeDtypeStruct((TOK, 8 * WIDE), B...  61.8 us
    unnamed x7, local copies, waits for them, and re-layouts  3.93 us

profile of v3, /device:TPU:48, one launch (start us, length us, event | category | flops | bytes accessed | tf_op | source)
XLA Modules:
  0.0 66.4 jit_solution(5565074390532976479)
XLA Ops:
  0.6 61.8 %attention_backward.1 = (bf16[128,4096]{1,0:T(8,128)(2,1)}, bf16[128,512]{1,0:T(8,128)(2,1)}, bf16[128,512]{1,0:T(8,128)(2,1)}) custom-call(bf16[128,4096]{1,0:T(8,128)(2,1)} %bitcast.14, bf16[128,512]{1,0:T(8,128)(2,1)} %bitcast.18, bf16[128,512]{1,0:T(8,128)(2,1)} %bitcast.19, bf16[128,4096]{1,0:T(8,128)(2,1)} %bitcast.15, f32[32,128]{1,0:T(8,128)} %bitcast.20, ...), custom_call_target="tpu_custom_call" | custom-call | tf_op jit(solution)/shard_map/attention_backward/pallas_call | solution.py:461
  62.5 0.0 copy-start.1
  62.5 2.3 %copy.13 = bf16[1,128,4096]{2,1,0:T(8,128)(2,1)} copy(bf16[1,128,4096]{2,1,0:T(8,128)(2,1)} %bitcast.13) | data formatting | bytes 2097152
  64.8 0.0 copy-done.1
  64.8 0.0 copy-start
  64.8 0.7 copy.14
  65.5 0.3 copy-done
  65.8 0.7 copy.15
Async XLA Ops:
  62.5 2.3 %copy-start.1 = (bf16[128,512]{1,0:T(8,128)(2,1)S(1)}, bf16[128,512]{1,0:T(8,128)(2,1)}, u32[]{:S(2)}) copy-start(bf16[128,512]{1,0:T(8,128)(2,1)} %get-tuple-element.7) | copy-start | bytes 393220
  64.8 1.0 %copy-start = (bf16[128,512]{1,0:T(8,128)(2,1)S(1)}, bf16[128,512]{1,0:T(8,128)(2,1)}, u32[]{:S(2)}) copy-start(bf16[128,512]{1,0:T(8,128)(2,1)} %get-tuple-element.8) | copy-start | bytes 393220

commit v4 on v3

--- a/solution.py
+++ b/solution.py
@@ -297,9 +297,9 @@
 
     @pl.loop(0, 12)
     def _(s):
-        from1, from4, from8, from9, from10 = ((s + 12 - n) // 12 for n in (1, 4, 8, 9, 10))
-        dz = from1 + from4 - from8 - from9
-        turn = from1 * (s - 1) - 3 * from4 - from8 - from9 - 3 * from10
+        from1, from4, from7, from8, from9, from10, from11 = ((s + 12 - n) // 12 for n in (1, 4, 7, 8, 9, 10, 11))
+        dz = from1 + from4 - 2 * from7 + 2 * from8 - 2 * from9 + from10 - from11
+        turn = from1 * (s - 1) - 3 * from4 - 2 * from7 + from8 - from9 - from10 - 2 * from11
         yq = (y + turn + turn // 2 - 2 * (turn // 3)) % 4
         is0, is2 = (2 - dz) // 2, dz // 2
         first = is2 * yq
@@ -334,7 +334,7 @@
 
         pl.when(((s < 2) | (s == 4)) & (z >= dz))(lambda: prepare_keys(dz))
 
-        @pl.when((s == 0) | (s == 2) | (s == 3) | (s == 7))
+        @pl.when((s == 0) | (s == 2) | (s == 3) | (s == 8))
         def _():
             @pl.when(s == 0)
             def _():
@@ -359,34 +359,32 @@
 
         pl.when(count % 2 == 1)(lambda: work(dz, [first + count - 1], yq))
 
-        @pl.when((s == 7) & (z > 1))
+        @pl.when((s == 8) & (z > 1))
         def _():
             share(2).start()
 
-        @pl.when((s == 8) & (z > 0))
-        def _():
-            share(1).start()
-
-            @pl.when(z > 1)
-            def _():
-                join(2)
-                for column in range(4):
-                    pass_down(2, column)
-
-        pl.when((s == 9) & (z > 0))(lambda: join(1))
-
-        @pl.when((s == 10) & (z > 0))
+        pl.when((s == 10) & (z > 0))(lambda: share(1).start())
+
+        @pl.when((s == 9) & (z > 1))
+        def _():
+            join(2)
+            for column in range(4):
+                pass_down(2, column)
+
+        pl.when((s == 11) & (z > 0))(lambda: join(1))
+
+        pl.when(s == 11)(lambda: share(0).start())
+
+        @pl.when((s == 4) | (s == 7) | (s >= 10))
+        def _():
+            finish_queries(yq)
+
+        @pl.when((s == 11) & (z > 0))
         def _():
             @pl.loop(0, 4)
             def _(column):
                 pl.when(z < 3)(lambda: join_above(1, column))
                 pass_down(1, column)
-
-        pl.when(s == 11)(lambda: share(0).start())
-
-        @pl.when((s == 4) | (s >= 9))
-        def _():
-            finish_queries(yq)
 
 
     def fin_keep(part):

time: 66.6 us -> 66.3 us (level)
  the two profiles are of different devices: /device:TPU:48 before, /device:TPU:219 now
where the time goes in v4:
time: 66.3 us; the launch traced here: 66.1 us
  Pallas kernels  61.6 us (93%)
  local copies, waits for them, and re-layouts  3.93 us (6%)
    pallas_call x1, Pallas kernels, on_device(): pl.pallas_call(kernel, out_shape=(jax.ShapeDtypeStruct((TOK, 8 * WIDE), B...  61.6 us
    unnamed x7, local copies, waits for them, and re-layouts  3.93 us

profile of v4, /device:TPU:219, one launch (start us, length us, event | category | flops | bytes accessed | tf_op | source)
XLA Modules:
  0.0 66.1 jit_solution(16992557899644552360)
XLA Ops:
  0.6 61.6 %attention_backward.1 = (bf16[128,4096]{1,0:T(8,128)(2,1)}, bf16[128,512]{1,0:T(8,128)(2,1)}, bf16[128,512]{1,0:T(8,128)(2,1)}) custom-call(bf16[128,4096]{1,0:T(8,128)(2,1)} %bitcast.14, bf16[128,512]{1,0:T(8,128)(2,1)} %bitcast.18, bf16[128,512]{1,0:T(8,128)(2,1)} %bitcast.19, bf16[128,4096]{1,0:T(8,128)(2,1)} %bitcast.15, f32[32,128]{1,0:T(8,128)} %bitcast.20, ...), custom_call_target="tpu_custom_call" | custom-call | tf_op jit(solution)/shard_map/attention_backward/pallas_call | solution.py:459
  62.2 0.0 copy-start.1
  62.2 2.3 %copy.13 = bf16[1,128,4096]{2,1,0:T(8,128)(2,1)} copy(bf16[1,128,4096]{2,1,0:T(8,128)(2,1)} %bitcast.13) | data formatting | bytes 2097152
  64.5 0.0 copy-done.1
  64.5 0.0 copy-start
  64.5 0.7 copy.14
  65.2 0.3 copy-done
  65.5 0.7 copy.15
Async XLA Ops:
  62.2 2.3 %copy-start.1 = (bf16[128,512]{1,0:T(8,128)(2,1)S(1)}, bf16[128,512]{1,0:T(8,128)(2,1)}, u32[]{:S(2)}) copy-start(bf16[128,512]{1,0:T(8,128)(2,1)} %get-tuple-element.7) | copy-start | bytes 393220
  64.5 1.0 %copy-start = (bf16[128,512]{1,0:T(8,128)(2,1)S(1)}, bf16[128,512]{1,0:T(8,128)(2,1)}, u32[]{:S(2)}) copy-start(bf16[128,512]{1,0:T(8,128)(2,1)} %get-tuple-element.8) | copy-start | bytes 393220
